TPU v7x, 32 devices: a whole 2x2x4 slice. The times are simulated.
32 devices in a mesh: freq: 4 (over x, core), vis: 8 (over z, y).
Axes of the slice: x: 2, y: 2, z: 4, core: 2. Of those that a mesh axis runs over, the one named last changes fastest.
Arguments:
- model_input: bfloat16 [2, 16, 512, 512], P(None, 'freq', 'vis'), parts along dimension 1, may hold values from -6 to 6
- w_kernels: bfloat16 [64, 2, 128, 128], P('freq'), parts along dimension 0, may hold values from -0.375 to 0.375
- visibilities: bfloat16 [1024, 2, 128, 128], P(('freq', 'vis')), parts along dimension 0, may hold values from -6 to 6
- tile_facet: int32 [1024], P(('freq', 'vis')), parts along dimension 0, may hold values from 0 to 3
- tile_patch: int32 [1024], P(('freq', 'vis')), parts along dimension 0, may hold values from 0 to 15
- tile_wplane: int32 [1024], P(('freq', 'vis')), parts along dimension 0, may hold values from 0 to 15
- tile_count: int32 [32], P(('freq', 'vis')), parts along dimension 0, may hold values from 16 to 32, as said below
Outputs:
- residual_image: float32 [16, 512, 512], P('freq', 'vis'), parts along dimension 0
There are 4 independent parts, one for each index of `freq`. A program takes and returns all parts, laid end to end along the dimension named above; each array names one. Nothing has to cross between parts.
Inputs may be any that keep to these rules, and one draw needn't show every extreme that they name: `tile_count`: each device's live tiles fill its first slots; some device holds exactly 32.
All inputs are finite; a program needn't handle non-finite values.
Results may differ from a plain program's by a relative error of at most 0.02.
Values may be sent and summed in bfloat16 or wider, within the bound.
No kernel may reach another device: no remote copies, remote signals or barrier semaphores. Data moves between devices by JAX's collectives and lax.ppermute only.
A program may use at most 128 MiB of HBM per device.

v0:
```python
import functools
import math

import jax
import jax.numpy as jnp
import ml_dtypes
import numpy as np
from jax import lax
from jax.experimental import pallas as pl
from jax.experimental.pallas import tpu as pltpu
from jax.sharding import PartitionSpec as P

P_SIZE = 512
S = 128
F = 4
WPLANES = 16
TILE_CAP = 32
NP = 16
SIDE = P_SIZE // S
PAIR = 2 * S
UNROLL = 6
PREP_UNROLL = 8
FIRST = 2
LISTS = F - FIRST + 1
SPARE = FIRST * NP
GAIN = 0.5
VMEM_BYTES = 60 * 1024 * 1024
LATER_VMEM = 52 * 1024 * 1024
FINAL_VMEM = 6 * 1024 * 1024

BF16 = jnp.bfloat16
F32 = jnp.float32


def angle_tables():
    index = np.arange(P_SIZE)
    angles = (index[:, None] * index[None, :] % P_SIZE) * (2.0 * np.pi / P_SIZE)
    return np.cos(angles) / np.sqrt(P_SIZE), np.sin(angles) / np.sqrt(P_SIZE)


def half(array):
    return np.asarray(array, np.float32).astype(ml_dtypes.bfloat16)


def complex_block(real, imag):
    return np.block([[real, -imag], [imag, real]])


def by_columns(table):
    rows, columns = table.shape
    return table.reshape(rows, columns // S, S).transpose(1, 0, 2)


def wide(ref, chunk):
    return jnp.concatenate([ref[chunk], ref[chunk + 1]], axis=1)


def row_table():
    cosine, sine = angle_tables()
    parts = [cosine.reshape(P_SIZE, SIDE, 1, S), -sine.reshape(P_SIZE, SIDE, 1, S)]
    return half(by_columns(np.concatenate(parts, axis=2).reshape(P_SIZE, 2 * P_SIZE)))


def column_tables(devices):
    cosine, sine = angle_tables()
    rows = P_SIZE // devices
    parts = [t.reshape(P_SIZE, devices, rows).transpose(1, 0, 2) for t in (cosine, sine)]
    return half(np.concatenate(parts, axis=2))


def flip_tables():
    small = np.zeros((S, S))
    for k in range(1, S):
        small[S - k, k] = 1.0
    zero = np.zeros((S, S))
    lanes = np.block([[small, zero], [zero, -small]])
    rows = np.zeros((PAIR, PAIR))
    for i in range(1, PAIR):
        rows[i, PAIR - i] = 1.0
    return half(by_columns(lanes)), half(by_columns(rows))


def inverse_row_tables():
    a, i = np.arange(S)[:, None], np.arange(S)[None, :]
    blocks = []
    for q in range(SIDE):
        angles = ((SIDE * a + q) * i % P_SIZE) * (2.0 * np.pi / P_SIZE)
        blocks.append(by_columns(complex_block(np.cos(angles), np.sin(angles)) / np.sqrt(P_SIZE)))
    return half(np.concatenate(blocks))


def inverse_column_table(weight):
    cosine, sine = angle_tables()
    parts = [cosine.reshape(SIDE, 1, S, P_SIZE), -sine.reshape(SIDE, 1, S, P_SIZE)]
    return half(by_columns(np.concatenate(parts, axis=1).reshape(2 * P_SIZE, P_SIZE) * weight))


def dot(a, b):
    return jnp.dot(a, b, preferred_element_type=F32)


def restack(pair):
    top = jnp.concatenate([pair[:S, :S], pair[S:, :S]], axis=1)
    bottom = jnp.concatenate([pair[:S, S:], pair[S:, S:]], axis=1)
    return jnp.concatenate([top, bottom], axis=0)


def turn_pair(pair):
    return jnp.concatenate([pair[:, :S], pair[:, S:]], axis=0)


def prepare(slot_ref, plane_ref, count_ref, wk_ref, vis_ref, sky_ref, row_ref, gram_ref, half_ref, kern, kern_t, acc, held, loads, leave):
    acc[...] = jnp.zeros_like(acc)
    loads[0].wait()
    for load in loads[4:]:
        load.start()
    for w in range(WPLANES):
        real, imag = wk_ref[w, 0], wk_ref[w, 1]
        block = jnp.concatenate(
            [jnp.concatenate([real, -imag], axis=1), jnp.concatenate([imag, real], axis=1)], axis=0
        )
        real_t, imag_t = real.T, imag.T
        block_t = jnp.concatenate(
            [jnp.concatenate([real_t, imag_t], axis=1), jnp.concatenate([-imag_t, real_t], axis=1)], axis=0
        )
        kern[w] = block
        kern_t[w] = block_t
        gram_ref[w] = dot(block_t, block).astype(BF16)
    leave[0].start()

    loads[1].wait()
    loads[2].wait()
    for pc in range(SIDE):
        half_ref[:, pc * PAIR : (pc + 1) * PAIR] = dot(sky_ref[...], wide(row_ref, 2 * pc)).astype(BF16)
    leave[1].start()

    loads[3].wait()
    count = count_ref[0]

    def right_product(n, lane):
        t = jnp.minimum(n * PREP_UNROLL + lane, TILE_CAP - 1)
        alive = jnp.where(n * PREP_UNROLL + lane < count, 1.0, 0.0).astype(F32)
        observed = jnp.concatenate([vis_ref[t, 0], vis_ref[t, 1]], axis=1)
        right = (dot(observed, kern[plane_ref[t]]) * alive).astype(BF16)
        held[lane, :, :S] = turn_pair(right)

    def left_product(n, lane):
        t = jnp.minimum(n * PREP_UNROLL + lane, TILE_CAP - 1)
        slot = slot_ref[t]
        both = dot(kern_t[plane_ref[t]], held[lane, :, :S])
        acc[slot] = acc[slot] + jnp.concatenate([both[:S], both[S:]], axis=1)

    def step(n, carry):
        for lane in range(PREP_UNROLL):
            left_product(n - 1, lane)
            right_product(n, lane)
        return carry

    batches = jnp.maximum((count + PREP_UNROLL - 1) // PREP_UNROLL, 1)
    for lane in range(PREP_UNROLL):
        right_product(0, lane)
    lax.fori_loop(1, batches, step, 0)
    for lane in range(PREP_UNROLL):
        left_product(batches - 1, lane)


def degrid_grid(items_ref, base, times, count, gram_ref, grid_ref, acc, held):
    def right_product(n, lane):
        code = items_ref[base + n * UNROLL + lane]
        first, second = (code >> 4) & (SPARE - 1), (code >> 10) & (SPARE - 1)
        pair = jnp.concatenate([grid_ref[first], grid_ref[second]], axis=0)
        right = dot(pair, gram_ref[code & (WPLANES - 1)])
        equal = items_ref[times + base + n * UNROLL + lane]
        right = [right[:S] * (equal & 0xFFFF).astype(F32), right[S:] * (equal >> 16).astype(F32)]
        held[lane] = restack(jnp.concatenate(right, axis=0).astype(BF16))

    def left_product(n, lane):
        code = items_ref[base + n * UNROLL + lane]
        both = dot(gram_ref[code & (WPLANES - 1)], held[lane])
        for k, slot in enumerate(((code >> 4) & 63, (code >> 10) & 63)):
            cols = slice(k * S, (k + 1) * S)
            acc[slot] = acc[slot] - jnp.concatenate([both[:S, cols], both[S:, cols]], axis=1)

    def step(n, carry):
        for lane in range(UNROLL):
            left_product(n - 1, lane)
            right_product(n, lane)
        return carry

    batches = jnp.maximum((count + UNROLL - 1) // UNROLL, 1)
    for lane in range(UNROLL):
        right_product(0, lane)
    lax.fori_loop(1, batches, step, 0)
    for lane in range(UNROLL):
        left_product(batches - 1, lane)


def both_cycles(
    facets, coef, base, times, count, pos, devices, items_ref, gram_ref, back_ref, half_of, tables, grid, acc, flip, held, keep_ref, send_ref
):
    column_ref, lanes_ref, rows_ref, inv_row_ref, inv_col_ref = tables[:5]
    loads = tables[5]

    def block(ref, facet, pc):
        first = facet * NP + pc * SIDE
        return ref[first : first + SIDE].reshape(P_SIZE, PAIR)

    def column_pass(cycle, facet, pc):
        part = half_of(cycle, facet, pc)
        turned = jnp.concatenate([part[:, S:], -part[:, :S]], axis=1)
        return dot(column_ref[...], jnp.concatenate([part, turned], axis=0))

    def place(ref, facet, pc, value):
        first = facet * NP + pc * SIDE
        ref[first : first + SIDE] = value.reshape(SIDE, S, PAIR)

    loads[1].wait()
    for facet in range(facets):
        for pc in range(SIDE):
            place(grid, facet, pc, column_pass(0, facet, pc).astype(BF16))
    if loads[0] is not None:
        loads[7].wait()
        acc[:NP] = back_ref[...].astype(F32)
        loads[0].wait()
    degrid_grid(items_ref, base, times, count, gram_ref, grid, acc, held)

    for load in loads[2:5]:
        if load is not None:
            load.wait()
    lane = lax.broadcasted_iota(jnp.int32, (1, PAIR), 1)
    row = lax.broadcasted_iota(jnp.int32, (PAIR, 1), 0)
    sign = jnp.where(lane < S, 1.0, -1.0).astype(F32)
    for facet in range(facets):
        for pc in range(SIDE):
            place(flip, facet, pc, block(acc, facet, pc).astype(BF16))
        for pc in range(SIDE):
            turned = dot(block(flip, facet, SIDE - 1 - pc), wide(lanes_ref, 0))
            edge = block(flip, facet, (SIDE - pc) % SIDE).astype(F32) * sign
            mirrored = jnp.where(lane % S == 0, edge, turned)
            mirrored_half = mirrored.astype(BF16)
            fresh = column_pass(1, facet, pc)
            own = block(acc, facet, pc)
            parts = []
            for b in range(2):
                mine = slice(b * PAIR, (b + 1) * PAIR)
                other = slice((1 - b) * PAIR, (2 - b) * PAIR)
                swapped = dot(wide(rows_ref, 0), mirrored_half[other])
                swapped = jnp.where(row == 0, mirrored[mine], swapped)
                parts.append((fresh[mine] + coef * (own[mine] + swapped)).astype(BF16))
            place(grid, facet, pc, jnp.concatenate(parts, axis=0))
    for facet in range(facets):
        for pc in range(SIDE):
            place(acc, facet, pc, block(back_ref, facet, pc).astype(F32))
    degrid_grid(items_ref, base, times, count, gram_ref, grid, acc, held)

    loads[5].wait()
    loads[6].wait()
    share, far = S // devices, devices // 2
    for facet in range(facets):
        mixed = [[] for _ in range(SIDE)]
        for pc in range(SIDE):
            r0, r1, r2, r3 = (acc[facet * NP + pc * SIDE + p] for p in range(SIDE))
            even, odd = r0 + r2, r0 - r2
            even_b, odd_b = r1 + r3, r1 - r3
            turned = jnp.concatenate([-odd_b[:, S:], odd_b[:, :S]], axis=1)
            for q, value in enumerate((even + even_b, odd + turned, even - even_b, odd - turned)):
                mixed[q].append(turn_pair(value.astype(BF16)))
        for q in range(SIDE):
            spec = dot(wide(inv_row_ref, 2 * q), jnp.concatenate(mixed[q], axis=1)).astype(BF16)
            for pc in range(SIDE):
                cols = slice(pc * S, (pc + 1) * S)
                flip[facet * NP + pc * SIDE + q] = jnp.concatenate([spec[:S, cols], spec[S:, cols]], axis=1)
        spec = jnp.concatenate([block(flip, facet, pc) for pc in range(SIDE)], axis=1)
        image = jnp.concatenate([dot(spec, wide(inv_col_ref, j)) for j in range(0, SIDE, 2)], axis=1).astype(BF16)
        for q in range(SIDE):
            part = image[q * S : (q + 1) * S]
            if send_ref is None:
                keep_ref[facet, q] = part
                continue
            odd, mine = pos & 1, pos >> 1
            for there in range(far):
                zero = part[2 * there * share : (2 * there + 1) * share]
                one = part[(2 * there + 1) * share : (2 * there + 2) * share]
                offset = there ^ mine
                keep_ref[offset, facet, q] = jnp.where(odd == 0, zero, one)
                send_ref[offset, facet, q] = jnp.where(odd == 0, one, zero)


def copies(moves, sems, first=0):
    return [pltpu.make_async_copy(src, dst, sems.at[first + k]) for k, (src, dst) in enumerate(moves)]


def first_kernel(facets, times, rows, coef, devices, outs, *refs):
    pos_ref, items_ref, slot_ref, plane_ref, live_ref = refs[:5]
    wk_hbm, vis_hbm, sky_hbm, row_hbm, column_hbm, *table_hbm = refs[5:14]
    gram_hbm, back_hbm, half_hbm, *images = refs[14 : 17 + outs]
    wk_ref, vis_ref, sky_ref, row_ref, column_ref, *table_refs = refs[17 + outs : 26 + outs]
    gram_ref, half_ref, back_ref, kern, kern_t, acc, grid, flip, held, sems = refs[26 + outs :]
    moves = [(wk_hbm, wk_ref), (sky_hbm, sky_ref), (row_hbm, row_ref), (vis_hbm, vis_ref), (column_hbm.at[pos_ref[0]], column_ref)]
    loads = copies(moves + list(zip(table_hbm, table_refs)), sems)
    for load in loads[:4]:
        load.start()
    later = facets * NP
    leave = copies(
        [(gram_ref, gram_hbm), (half_ref, half_hbm), (back_ref.at[pl.ds(later, F * NP - later)], back_hbm)], sems, len(loads)
    )
    prepare(
        slot_ref, plane_ref, live_ref, wk_ref, vis_ref, sky_ref, row_ref, gram_ref, half_ref, kern, kern_t, acc, held, loads, leave
    )
    for slot in range(0, F * NP, NP):
        back_ref[slot : slot + NP] = acc[slot : slot + NP].astype(BF16)
    leave[2].start()

    def half_of(cycle, facet, pc):
        first = (cycle * F + facet) * rows
        return half_ref[first : first + rows, pc * PAIR : (pc + 1) * PAIR]

    tables = (column_ref, *table_refs, [None, loads[4], None, *loads[5:]])
    keep_ref, send_ref = images if outs == 2 else (images[0], None)
    both_cycles(
        facets, coef, 0, times, items_ref[2 * times], pos_ref[0], devices, items_ref, gram_ref, back_ref, half_of, tables, grid, acc, flip, held, keep_ref, send_ref
    )
    for out in leave:
        out.wait()


def later_kernel(facet, offset, base, times, part, rows, coef, devices, outs, *refs):
    pos_ref, items_ref = refs[:2]
    gram_hbm, back_hbm, half_hbm, column_hbm, *table_hbm = refs[2:10]
    images = refs[10 : 10 + outs]
    gram_ref, back_ref, half_ref, column_ref, *table_refs = refs[10 + outs : 18 + outs]
    acc, grid, flip, held, sems = refs[18 + outs :]
    moves = [
        (half_hbm.at[pl.ds(facet * rows, rows)], half_ref.at[0]),
        (column_hbm.at[pos_ref[0]], column_ref),
        (back_hbm.at[pl.ds(offset, NP)], back_ref),
        (gram_hbm, gram_ref),
        (half_hbm.at[pl.ds((F + facet) * rows, rows)], half_ref.at[1]),
    ]
    loads = copies(moves + list(zip(table_hbm, table_refs)), sems)
    for load in loads[:4]:
        load.start()
    for load in loads[4:]:
        load.start()
    loads[0].wait()

    def half_of(cycle, _, pc):
        return half_ref[cycle, :, pc * PAIR : (pc + 1) * PAIR]

    tables = (column_ref, *table_refs, [loads[3], loads[1], *loads[4:], loads[2]])
    keep_ref, send_ref = images if outs == 2 else (images[0], None)
    both_cycles(
        1, coef, base, times, items_ref[2 * times + part], pos_ref[0], devices, items_ref, gram_ref, back_ref, half_of, tables, grid, acc, flip, held, keep_ref, send_ref
    )


def tile_lists(codes, stride):
    total = codes.shape[0]
    ids = jnp.arange(total, dtype=jnp.int32)
    before = ids[None, :] < ids[:, None]
    equal = codes[:, None] == codes[None, :]
    again = jnp.sum((equal & before).astype(jnp.int32), axis=1) > 0
    times = jnp.sum(equal.astype(jnp.int32), axis=1)
    group = jnp.where(again, LISTS * WPLANES, codes >> 6)
    rank = jnp.sum(((group[:, None] == group[None, :]) & before).astype(jnp.int32), axis=1)
    planes = jnp.arange(LISTS * WPLANES, dtype=jnp.int32)
    pairs = (jnp.sum((group[None, :] == planes[:, None]).astype(jnp.int32), axis=1) + 1) >> 1
    which = group >> 4
    earlier = (planes[None, :] < group[:, None]) & ((planes[None, :] >> 4) == which[:, None])
    base = jnp.sum(jnp.where(earlier, pairs[None, :], 0), axis=1)
    where = which * stride + base + (rank >> 1)
    slot, plane = codes & 63, (codes >> 6) & (WPLANES - 1)
    even = (rank & 1) == 0
    delta = jnp.where(even, plane + ((slot - SPARE) << 4), (slot - SPARE) << 10)
    size = LISTS * stride
    places = jnp.arange(2 * size + LISTS, dtype=jnp.int32)[:, None]
    is_item, is_times = places < size, places < 2 * size
    goal = jnp.where(is_item, places, jnp.where(is_times, places - size, places - 2 * size))
    hit = (goal == jnp.where(is_times, where[None, :], which[None, :])) & (which < LISTS)[None, :]
    times = jnp.where(even, times, times << 16)
    value = jnp.where(is_item, delta[None, :], jnp.where(is_times, times[None, :], even.astype(jnp.int32)[None, :]))
    dummy = jnp.where(places[:, 0] < size, (SPARE << 4) + (SPARE << 10), 0)
    return dummy + jnp.sum(jnp.where(hit, value, 0), axis=1)


def exchange(value, bits, devices):
    return lax.ppermute(value, "vis", [(i, i ^ bits) for i in range(devices)])


def split_image(image, position, devices):
    share, far = S // devices, devices // 2
    parts = image.reshape(-1, SIDE, far, 2, share, P_SIZE).transpose(3, 2, 0, 1, 4, 5)
    parts = jnp.take(parts, jnp.arange(far) ^ (position >> 1), axis=1)
    odd = position & 1
    return lax.dynamic_index_in_dim(parts, odd, 0, False), lax.dynamic_index_in_dim(parts, 1 - odd, 0, False)


def merge(arrays, first, last):
    parts = [a[first:last].astype(F32) for a in arrays if a.shape[0] >= last]
    return functools.reduce(jnp.add, parts).astype(BF16)


def final_kernel(groups, *refs):
    out_ref, mixed = refs[-2:]
    f = first = 0
    for parts in groups:
        for k in range(refs[first].shape[1]):
            for q in range(SIDE):
                total = functools.reduce(jnp.add, [ref[0, k, q].astype(F32) for ref in refs[first : first + parts]])
                for c in range(SIDE):
                    mixed[f, c, pl.ds(q, total.shape[0], stride=SIDE), :] = total[:, c * S : (c + 1) * S]
            for c in range(SIDE):
                out_ref[f, :, c * S : (c + 1) * S] = mixed[f, c]
            f += 1
        first += parts


def local(model_input, w_kernels, visibilities, tile_facet, tile_patch, tile_wplane, tile_count):
    devices = lax.axis_size("vis")
    position = lax.axis_index("vis").astype(jnp.int32)
    rows = P_SIZE // devices
    weight = math.sqrt(F * NP / (TILE_CAP * devices))
    total = TILE_CAP * devices
    stride = total // 2 + WPLANES // 2 + UNROLL
    coef = GAIN * weight / 2

    slots = tile_facet * NP + (tile_patch & 3) * SIDE + (tile_patch >> 2)
    live = jnp.arange(TILE_CAP, dtype=jnp.int32) < tile_count[0]
    which = jnp.maximum(tile_facet - (FIRST - 1), 0)
    near = jnp.where(tile_facet < FIRST, slots, slots & (NP - 1))
    codes = jnp.where(live, (which << 10) + (tile_wplane << 6) + near, LISTS << 10)
    bits = 1
    while bits < devices:
        codes = jnp.concatenate([codes, exchange(codes, bits, devices)])
        bits *= 2
    items = tile_lists(codes, stride)

    lanes, row_flip = flip_tables()
    tables = [column_tables(devices), lanes, row_flip, inverse_row_tables(), inverse_column_table(weight)]
    tables = [jnp.asarray(t) for t in tables]
    here = position.reshape(1)
    smem = pl.BlockSpec(memory_space=pltpu.SMEM)
    vmem = pl.BlockSpec(memory_space=pltpu.VMEM)
    hbm = pl.BlockSpec(memory_space=pl.ANY)
    share, far = S // devices, devices // 2
    split = share % 16 == 0

    def image_shapes(facets):
        if split:
            return [jax.ShapeDtypeStruct((far, facets, SIDE, share, P_SIZE), BF16)] * 2
        return [jax.ShapeDtypeStruct((facets, SIDE, S, P_SIZE), BF16)]

    def halves_of(images):
        return images if split else split_image(images[0], position, devices)

    params = pltpu.CompilerParams(vmem_limit_bytes=VMEM_BYTES)
    outs = 2 if split else 1
    half_shape = (2 * F * rows, 2 * P_SIZE)
    gram_shape = (WPLANES, PAIR, PAIR)
    table_scratch = [pltpu.VMEM((P_SIZE, 2 * rows), BF16)] + [pltpu.VMEM(t.shape, BF16) for t in tables[1:]]

    gram, back, half_rows, *images = pl.pallas_call(
        functools.partial(first_kernel, FIRST, LISTS * stride, rows, coef, devices, outs),
        out_shape=[
            jax.ShapeDtypeStruct(gram_shape, BF16),
            jax.ShapeDtypeStruct(((F - FIRST) * NP, S, PAIR), BF16),
            jax.ShapeDtypeStruct(half_shape, BF16),
            *image_shapes(FIRST),
        ],
        in_specs=[smem] * 5 + [hbm] * 9,
        out_specs=[hbm] * 3 + [vmem] * outs,
        scratch_shapes=[
            pltpu.VMEM(w_kernels.shape, BF16),
            pltpu.VMEM(visibilities.shape, BF16),
            pltpu.VMEM((2 * F * rows, P_SIZE), BF16),
            pltpu.VMEM((2 * SIDE, P_SIZE, S), BF16),
            *table_scratch,
            pltpu.VMEM(gram_shape, BF16),
            pltpu.VMEM(half_shape, BF16),
            pltpu.VMEM((F * NP, S, PAIR), BF16),
            pltpu.VMEM(gram_shape, BF16),
            pltpu.VMEM(gram_shape, BF16),
            pltpu.VMEM((F * NP + 1, S, PAIR), F32),
            pltpu.VMEM((FIRST * NP, S, PAIR), BF16),
            pltpu.VMEM((FIRST * NP, S, PAIR), BF16),
            pltpu.VMEM((max(UNROLL, PREP_UNROLL), PAIR, PAIR), BF16),
            pltpu.SemaphoreType.DMA((12,)),
        ],
        compiler_params=params,
        cost_estimate=pl.CostEstimate(flops=30 * 10**9, bytes_accessed=12 * 2**20, transcendentals=0),
        name="first",
    )(
        here,
        items,
        slots,
        tile_wplane,
        tile_count,
        w_kernels,
        visibilities,
        model_input.reshape(2 * F * rows, P_SIZE),
        jnp.asarray(row_table()),
        *tables,
    )

    keep, send = halves_of(images)
    arrays = [[keep, exchange(send, 1, devices)]]

    def halve(group, width):
        sent = merge(arrays[group], width, 2 * width)
        return sent, exchange(sent, 2 * width, devices)

    for facet in range(FIRST, F):
        part = facet - FIRST + 1
        if part == 2:
            width = far // 2
            sent, got = halve(0, width)
            here, _ = lax.optimization_barrier((here, sent))
        images = pl.pallas_call(
            functools.partial(
                later_kernel, facet, (facet - FIRST) * NP, part * stride, LISTS * stride, part, rows, coef, devices, outs
            ),
            out_shape=image_shapes(1),
            in_specs=[smem] * 2 + [hbm] * 8,
            out_specs=[vmem] * outs,
            scratch_shapes=[
                pltpu.VMEM(gram_shape, BF16),
                pltpu.VMEM((NP, S, PAIR), BF16),
                pltpu.VMEM((2, rows, 2 * P_SIZE), BF16),
                *table_scratch,
                pltpu.VMEM((SPARE + 1, S, PAIR), F32),
                pltpu.VMEM((NP, S, PAIR), BF16),
                pltpu.VMEM((NP, S, PAIR), BF16),
                pltpu.VMEM((max(UNROLL, PREP_UNROLL), PAIR, PAIR), BF16),
                pltpu.SemaphoreType.DMA((9,)),
            ],
            compiler_params=pltpu.CompilerParams(vmem_limit_bytes=LATER_VMEM),
            cost_estimate=pl.CostEstimate(flops=14 * 10**9, bytes_accessed=6 * 2**20, transcendentals=0),
            name="facet",
        )(here, items, gram, back, half_rows, *tables)
        keep, send = halves_of(images)
        if part == 2:
            send, got = lax.optimization_barrier((send, got))
            arrays[0].append(got)
        arrays.append([keep, exchange(send, 1, devices)])
    while width > 1:
        width //= 2
        arrays[0].append(halve(0, width)[1])
    for group in range(1, LISTS):
        arrays[group] += [exchange(merge(arrays[group], k, k + 1), 2 * k, devices) for k in range(1, far)]

    def finish(groups, first, facets, before):
        operands = [a for group in groups for a in arrays[group]]
        in_specs = [pl.BlockSpec((1,) + a.shape[1:], lambda i: (0, 0, 0, 0, 0)) for a in operands]
        aliases = {len(operands): 0} if before else {}
        return pl.pallas_call(
            functools.partial(final_kernel, [len(arrays[group]) for group in groups]),
            out_shape=jax.ShapeDtypeStruct((F, rows, P_SIZE), F32),
            grid=(1,),
            in_specs=in_specs + [hbm] * len(before),
            out_specs=pl.BlockSpec((facets, rows, P_SIZE), lambda i: (first // facets, 0, 0)),
            scratch_shapes=[pltpu.VMEM((facets, SIDE, rows, S), F32)],
            input_output_aliases=aliases,
            compiler_params=pltpu.CompilerParams(vmem_limit_bytes=FINAL_VMEM),
            cost_estimate=pl.CostEstimate(flops=10**6, bytes_accessed=2**20, transcendentals=0),
            name="final",
        )(*operands, *before)

    done = finish(range(LISTS - 1), 0, F - 1, [])
    return finish([LISTS - 1], F - 1, 1, [done])


def solution(mesh):
    return jax.shard_map(
        local,
        mesh=mesh,
        in_specs=(
            P(None, "freq", "vis", None),
            P("freq", None, None, None),
            P(("freq", "vis"), None, None, None),
            P(("freq", "vis")),
            P(("freq", "vis")),
            P(("freq", "vis")),
            P(("freq", "vis")),
        ),
        out_specs=P("freq", "vis", None),
        check_vma=False,
    )
```

profile of v0, /device:TPU:0, one launch (start us, length us, event | category | flops | bytes accessed | tf_op | source)
XLA Modules:
  0.0 85.0 jit_solution(14385415822561535545)
XLA Ops:
  0.7 1.2 %shift-right-arithmetic_add_fusion.1 = (s32[32]{0:T(128)}, s32[32]{0:T(128)S(1)}) fusion(s32[32]{0:T(128)} %param.17, s32[32]{0:T(128)} %param.16, s32[32]{0:T(128)} %refs_3_.1, s32[]{:T(128)} %bitcast.3), kind=kLoop, calls=%fused_computation.45 | loop fusion | flops 544 | bytes 644 | tf_op jit(solution)/shard_map/add | solution.py:427
  1.9 3.0 %collective-permute-start = (s32[32]{0:T(128)S(1)}, s32[32]{0:T(128)S(1)}, u32[]{:S(2)}, u32[]{:S(2)}) collective-permute-start(s32[32]{0:T(128)S(1)} %get-tuple-element.40), channel_id=1, source_target_pairs={{0,1},{1,0},{2,3},{3,2},{4,5},{5,4},{6,7},{7,6},{8,9},{9,8},{10,11... | collective-permute-start | bytes 392 | tf_op jit(solution)/shard_map/ppermute | solution.py:387
  4.9 1.5 %collective-permute-done = s32[32]{0:T(128)S(1)} collective-permute-done((s32[32]{0:T(128)S(1)}, s32[32]{0:T(128)S(1)}, u32[]{:S(2)}, u32[]{:S(2)}) %collective-permute-start) | collective-permute-done | bytes 160 | tf_op jit(solution)/shard_map/ppermute | solution.py:387
  6.5 2.1 %collective-permute-start.1 = (s32[64]{0:T(128)S(1)}, s32[64]{0:T(128)S(1)}, u32[]{:S(2)}, u32[]{:S(2)}) collective-permute-start(s32[64]{0:T(128)S(1)} %pad_add_fusion.1), channel_id=1, source_target_pairs={{0,2},{1,3},{2,0},{3,1},{4,6},{5,7},{6,4},{7,5},{8,10},{9,11},{10,... | collective-permute-start | bytes 776 | tf_op jit(solution)/shard_map/ppermute | solution.py:387
  8.5 1.5 %collective-permute-done.1 = s32[64]{0:T(128)S(1)} collective-permute-done((s32[64]{0:T(128)S(1)}, s32[64]{0:T(128)S(1)}, u32[]{:S(2)}, u32[]{:S(2)}) %collective-permute-start.1) | collective-permute-done | bytes 288 | tf_op jit(solution)/shard_map/ppermute | solution.py:387
  10.1 3.0 %collective-permute-start.2 = (s32[128]{0:T(128)S(1)}, s32[128]{0:T(128)S(1)}, u32[]{:S(2)}, u32[]{:S(2)}) collective-permute-start(s32[128]{0:T(128)S(1)} %pad_add_fusion.2), channel_id=1, source_target_pairs={{0,4},{1,5},{2,6},{3,7},{4,0},{5,1},{6,2},{7,3},{8,12},{9,13},{10,... | collective-permute-start | bytes 1544 | tf_op jit(solution)/shard_map/ppermute | solution.py:387
  13.2 1.5 %collective-permute-done.2 = s32[128]{0:T(128)S(1)} collective-permute-done((s32[128]{0:T(128)S(1)}, s32[128]{0:T(128)S(1)}, u32[]{:S(2)}, u32[]{:S(2)}) %collective-permute-start.2) | collective-permute-done | bytes 544 | tf_op jit(solution)/shard_map/ppermute | solution.py:387
  16.6 22.8 %first.1 = (bf16[16,256,256]{2,1,0:T(8,128)(2,1)}, bf16[32,128,256]{2,1,0:T(8,128)(2,1)}, bf16[512,1024]{1,0:T(8,128)(2,1)}, bf16[4,2,4,16,512]{4,3,2,1,0:T(8,128)(2,1)}, bf16[4,2,4,16,512]{4,3,2,1,0:T(8,128)(2,1)}) custom-call(s32[1]{0:T(128)} %bitcast.refs_0_, s32[855]{0:T(1024)} %select_add_fusion.refs_1_, s32[32]{0:T(128)} %get-tuple-element.39.refs_2_, ...), custom_call_target="tpu_custom_call" | custom-call | flops 30000001024 | bytes 12582912 | tf_op jit(solution)/shard_map/first/pallas_call | solution.py:462
  39.4 2.5 %collective-permute-start.3 = (bf16[4,2,4,16,512]{4,3,2,1,0:T(8,128)(2,1)}, bf16[4,2,4,16,512]{4,3,2,1,0:T(8,128)(2,1)S(1)}, u32[]{:S(2)}, u32[]{:S(2)}) collective-permute-start(bf16[4,2,4,16,512]{4,3,2,1,0:T(8,128)(2,1)} %get-tuple-element.18), channel_id=1, source_target_pairs={{0,1},{1,0},{2,3},{3,2},{4,5},{5,4},{6,7},{7,6},{8,9},{9,8},{10,11... | collective-permute-start | bytes 1572872 | tf_op jit(solution)/shard_map/ppermute | solution.py:387
  41.9 11.7 %facet.3 = (bf16[4,1,4,16,512]{4,3,2,1,0:T(8,128)(2,1)S(1)}, bf16[4,1,4,16,512]{4,3,2,1,0:T(8,128)(2,1)S(1)}) custom-call(s32[1]{0:T(128)} %bitcast.refs_0_, s32[855]{0:T(1024)S(1)} %copy-done.1, bf16[16,256,256]{2,1,0:T(8,128)(2,1)} %get-tuple-element.20.refs_2_, bf16[32,128,256]{2,1,0:T(8,128)(2,1)} %get-tuple-element.21.refs_3_, ...), custom_call_target="tpu_custom_call" | custom-call | flops 14000000000 | bytes 6291456 | tf_op jit(solution)/shard_map/facet/pallas_call | solution.py:518
  53.8 2.6 %collective-permute-start.4 = (bf16[2,2,4,16,512]{4,3,2,1,0:T(8,128)(2,1)S(1)}, bf16[2,2,4,16,512]{4,3,2,1,0:T(8,128)(2,1)S(1)}, u32[]{:S(2)}, u32[]{:S(2)}) collective-permute-start(bf16[2,2,4,16,512]{4,3,2,1,0:T(8,128)(2,1)S(1)} %add_convert_fusion), channel_id=1, source_target_pairs={{0,4},{1,5},{2,6},{3,7},{4,0},{5,1},{6,2},{7,3},{8,12},{9,13},{10,... | collective-permute-start | bytes 786440 | tf_op jit(solution)/shard_map/ppermute | solution.py:387
  56.4 12.9 %facet.2 = (bf16[4,1,4,16,512]{4,3,2,1,0:T(8,128)(2,1)S(1)}, bf16[4,1,4,16,512]{4,3,2,1,0:T(8,128)(2,1)S(1)}) custom-call(s32[1]{0:T(128)} %bitcast.refs_0_, s32[855]{0:T(1024)S(1)} %copy-done.1, bf16[16,256,256]{2,1,0:T(8,128)(2,1)} %get-tuple-element.20.refs_2_, bf16[32,128,256]{2,1,0:T(8,128)(2,1)} %get-tuple-element.21.refs_3_, ...), custom_call_target="tpu_custom_call" | custom-call | flops 14000000000 | bytes 6291456 | tf_op jit(solution)/shard_map/facet/pallas_call | solution.py:518
  69.2 1.6 %collective-permute-start.5 = (bf16[4,1,4,16,512]{4,3,2,1,0:T(8,128)(2,1)S(1)}, bf16[4,1,4,16,512]{4,3,2,1,0:T(8,128)(2,1)S(1)}, u32[]{:S(2)}, u32[]{:S(2)}) collective-permute-start(bf16[4,1,4,16,512]{4,3,2,1,0:T(8,128)(2,1)S(1)} %get-tuple-element.25), channel_id=1, source_target_pairs={{0,1},{1,0},{2,3},{3,2},{4,5},{5,4},{6,7},{7,6},{8,9},{9,8},{10,11... | collective-permute-start | bytes 786440 | tf_op jit(solution)/shard_map/ppermute | solution.py:387
  70.9 2.0 %collective-permute-start.13 = (bf16[1,1,4,16,512]{4,3,2,1,0:T(8,128)(2,1)S(1)}, bf16[1,1,4,16,512]{4,3,2,1,0:T(8,128)(2,1)S(1)}, u32[]{:S(2)}, u32[]{:S(2)}) collective-permute-start(bf16[1,1,4,16,512]{4,3,2,1,0:T(8,128)(2,1)S(1)} %get-tuple-element.33), channel_id=1, source_target_pairs={{0,6},{1,7},{2,4},{3,5},{4,2},{5,3},{6,0},{7,1},{8,14},{9,15},{10,... | collective-permute-start | bytes 196616 | tf_op jit(solution)/shard_map/ppermute | solution.py:387
  72.9 1.7 %collective-permute-start.12 = (bf16[1,1,4,16,512]{4,3,2,1,0:T(8,128)(2,1)S(1)}, bf16[1,1,4,16,512]{4,3,2,1,0:T(8,128)(2,1)S(1)}, u32[]{:S(2)}, u32[]{:S(2)}) collective-permute-start(bf16[1,1,4,16,512]{4,3,2,1,0:T(8,128)(2,1)S(1)} %get-tuple-element.34), channel_id=1, source_target_pairs={{0,4},{1,5},{2,6},{3,7},{4,0},{5,1},{6,2},{7,3},{8,12},{9,13},{10,... | collective-permute-start | bytes 196616 | tf_op jit(solution)/shard_map/ppermute | solution.py:387
  74.6 0.8 collective-permute-start.11
  75.4 1.3 %collective-permute-start.9 = (bf16[1,2,4,16,512]{4,3,2,1,0:T(8,128)(2,1)S(1)}, bf16[1,2,4,16,512]{4,3,2,1,0:T(8,128)(2,1)S(1)}, u32[]{:S(2)}, u32[]{:S(2)}) collective-permute-start(bf16[1,2,4,16,512]{4,3,2,1,0:T(8,128)(2,1)S(1)} %add_convert_fusion.1), channel_id=1, source_target_pairs={{0,2},{1,3},{2,0},{3,1},{4,6},{5,7},{6,4},{7,5},{8,10},{9,11},{10,... | collective-permute-start | bytes 393224 | tf_op jit(solution)/shard_map/ppermute | solution.py:387
  76.8 1.0 %collective-permute-start.8 = (bf16[1,1,4,16,512]{4,3,2,1,0:T(8,128)(2,1)S(1)}, bf16[1,1,4,16,512]{4,3,2,1,0:T(8,128)(2,1)S(1)}, u32[]{:S(2)}, u32[]{:S(2)}) collective-permute-start(bf16[1,1,4,16,512]{4,3,2,1,0:T(8,128)(2,1)S(1)} %get-tuple-element.36), channel_id=1, source_target_pairs={{0,6},{1,7},{2,4},{3,5},{4,2},{5,3},{6,0},{7,1},{8,14},{9,15},{10,... | collective-permute-start | bytes 196616 | tf_op jit(solution)/shard_map/ppermute | solution.py:387
  77.8 1.3 %collective-permute-start.7 = (bf16[1,1,4,16,512]{4,3,2,1,0:T(8,128)(2,1)S(1)}, bf16[1,1,4,16,512]{4,3,2,1,0:T(8,128)(2,1)S(1)}, u32[]{:S(2)}, u32[]{:S(2)}) collective-permute-start(bf16[1,1,4,16,512]{4,3,2,1,0:T(8,128)(2,1)S(1)} %get-tuple-element.37), channel_id=1, source_target_pairs={{0,4},{1,5},{2,6},{3,7},{4,0},{5,1},{6,2},{7,3},{8,12},{9,13},{10,... | collective-permute-start | bytes 196616 | tf_op jit(solution)/shard_map/ppermute | solution.py:387
  79.1 2.1 %collective-permute-start.6 = (bf16[1,1,4,16,512]{4,3,2,1,0:T(8,128)(2,1)S(1)}, bf16[1,1,4,16,512]{4,3,2,1,0:T(8,128)(2,1)S(1)}, u32[]{:S(2)}, u32[]{:S(2)}) collective-permute-start(bf16[1,1,4,16,512]{4,3,2,1,0:T(8,128)(2,1)S(1)} %get-tuple-element.38), channel_id=1, source_target_pairs={{0,2},{1,3},{2,0},{3,1},{4,6},{5,7},{6,4},{7,5},{8,10},{9,11},{10,... | collective-permute-start | bytes 196616 | tf_op jit(solution)/shard_map/ppermute | solution.py:387
  81.2 0.9 %final.2.refs_5_ = f32[4,64,512]{2,1,0:T(8,128)} custom-call(bf16[4,2,4,16,512]{4,3,2,1,0:T(8,128)(2,1)S(1)} %copy-done, bf16[4,2,4,16,512]{4,3,2,1,0:T(8,128)(2,1)S(1)} %collective-permute-done.3.refs_1_, bf16[2,2,4,16,512]{4,3,2,1,0:T(8,128)(2,1)S(1)} %collective-permute-done.4.refs_2_, bf16[1,2,4,16,512]{4,3,2,1,0:T(8,128)(2,1)S(1)} %collective-permute-done.9.refs_3_, ...), custom_call_target="tpu_custom_call" | custom-call | flops 1000000 | bytes 1048576 | tf_op jit(solution)/shard_map/final/pallas_call | solution.py:555
  82.1 0.9 %collective-permute-done.8.refs_4_ = bf16[1,1,4,16,512]{4,3,2,1,0:T(8,128)(2,1)S(1)} collective-permute-done((bf16[1,1,4,16,512]{4,3,2,1,0:T(8,128)(2,1)S(1)}, bf16[1,1,4,16,512]{4,3,2,1,0:T(8,128)(2,1)S(1)}, u32[]{:S(2)}, u32[]{:S(2)}) %collective-permute-start.8) | collective-permute-done | bytes 65568 | tf_op jit(solution)/shard_map/ppermute | solution.py:387
  83.0 1.3 %collective-permute-done.7.refs_3_ = bf16[1,1,4,16,512]{4,3,2,1,0:T(8,128)(2,1)S(1)} collective-permute-done((bf16[1,1,4,16,512]{4,3,2,1,0:T(8,128)(2,1)S(1)}, bf16[1,1,4,16,512]{4,3,2,1,0:T(8,128)(2,1)S(1)}, u32[]{:S(2)}, u32[]{:S(2)}) %collective-permute-start.7) | collective-permute-done | bytes 65568 | tf_op jit(solution)/shard_map/ppermute | solution.py:387
  84.3 0.7 final.3
  (41 shorter events, 2.5 us)
Async XLA Ops:
  1.9 4.5 %collective-permute-start = (s32[32]{0:T(128)S(1)}, s32[32]{0:T(128)S(1)}, u32[]{:S(2)}, u32[]{:S(2)}) collective-permute-start(s32[32]{0:T(128)S(1)} %get-tuple-element.40), channel_id=1, source_target_pairs={{0,1},{1,0},{2,3},{3,2},{4,5},{5,4},{6,7},{7,6},{8,9},{9,8},{10,11... | collective-permute-start | bytes 392 | tf_op jit(solution)/shard_map/ppermute | solution.py:387
  6.5 3.6 %collective-permute-start.1 = (s32[64]{0:T(128)S(1)}, s32[64]{0:T(128)S(1)}, u32[]{:S(2)}, u32[]{:S(2)}) collective-permute-start(s32[64]{0:T(128)S(1)} %pad_add_fusion.1), channel_id=1, source_target_pairs={{0,2},{1,3},{2,0},{3,1},{4,6},{5,7},{6,4},{7,5},{8,10},{9,11},{10,... | collective-permute-start | bytes 776 | tf_op jit(solution)/shard_map/ppermute | solution.py:387
  10.1 4.6 %collective-permute-start.2 = (s32[128]{0:T(128)S(1)}, s32[128]{0:T(128)S(1)}, u32[]{:S(2)}, u32[]{:S(2)}) collective-permute-start(s32[128]{0:T(128)S(1)} %pad_add_fusion.2), channel_id=1, source_target_pairs={{0,4},{1,5},{2,6},{3,7},{4,0},{5,1},{6,2},{7,3},{8,12},{9,13},{10,... | collective-permute-start | bytes 1544 | tf_op jit(solution)/shard_map/ppermute | solution.py:387
  16.6 25.3 %copy-start.1 = (s32[855]{0:T(1024)S(1)}, s32[855]{0:T(1024)}, u32[]{:S(2)}) copy-start(s32[855]{0:T(1024)} %select_add_fusion.refs_1_) | copy-start | bytes 10264
  16.6 25.3 %copy-start.2 = (bf16[8,256,128]{2,1,0:T(8,128)(2,1)S(1)}, bf16[8,256,128]{2,1,0:T(8,128)(2,1)}, u32[]{:S(2)}) copy-start(bf16[8,256,128]{2,1,0:T(8,128)(2,1)} %constant.25.clone.refs_12_.refs_8_) | copy-start | bytes 1572868
  16.6 25.3 %copy-start.3 = (bf16[2,256,128]{2,1,0:T(8,128)(2,1)S(1)}, bf16[2,256,128]{2,1,0:T(8,128)(2,1)}, u32[]{:S(2)}) copy-start(bf16[2,256,128]{2,1,0:T(8,128)(2,1)} %constant.24.clone.refs_11_.refs_7_) | copy-start | bytes 393220
  16.6 25.3 %copy-start.4 = (bf16[2,256,128]{2,1,0:T(8,128)(2,1)S(1)}, bf16[2,256,128]{2,1,0:T(8,128)(2,1)}, u32[]{:S(2)}) copy-start(bf16[2,256,128]{2,1,0:T(8,128)(2,1)} %constant.23.clone.refs_10_.refs_6_) | copy-start | bytes 393220
  39.4 14.3 %collective-permute-start.3 = (bf16[4,2,4,16,512]{4,3,2,1,0:T(8,128)(2,1)}, bf16[4,2,4,16,512]{4,3,2,1,0:T(8,128)(2,1)S(1)}, u32[]{:S(2)}, u32[]{:S(2)}) collective-permute-start(bf16[4,2,4,16,512]{4,3,2,1,0:T(8,128)(2,1)} %get-tuple-element.18), channel_id=1, source_target_pairs={{0,1},{1,0},{2,3},{3,2},{4,5},{5,4},{6,7},{7,6},{8,9},{9,8},{10,11... | collective-permute-start | bytes 1572872 | tf_op jit(solution)/shard_map/ppermute | solution.py:387
  41.9 11.8 %copy-start = (bf16[4,2,4,16,512]{4,3,2,1,0:T(8,128)(2,1)S(1)}, bf16[4,2,4,16,512]{4,3,2,1,0:T(8,128)(2,1)}, u32[]{:S(2)}) copy-start(bf16[4,2,4,16,512]{4,3,2,1,0:T(8,128)(2,1)} %get-tuple-element.17.refs_0_) | copy-start | bytes 1572868
  53.6 17.2 %collective-permute-start.10 = (bf16[4,1,4,16,512]{4,3,2,1,0:T(8,128)(2,1)S(1)}, bf16[4,1,4,16,512]{4,3,2,1,0:T(8,128)(2,1)S(1)}, u32[]{:S(2)}, u32[]{:S(2)}) collective-permute-start(bf16[4,1,4,16,512]{4,3,2,1,0:T(8,128)(2,1)S(1)} %get-tuple-element.28), channel_id=1, source_target_pairs={{0,1},{1,0},{2,3},{3,2},{4,5},{5,4},{6,7},{7,6},{8,9},{9,8},{10,11... | collective-permute-start | bytes 786440 | tf_op jit(solution)/shard_map/ppermute | solution.py:387
  53.8 15.4 %collective-permute-start.4 = (bf16[2,2,4,16,512]{4,3,2,1,0:T(8,128)(2,1)S(1)}, bf16[2,2,4,16,512]{4,3,2,1,0:T(8,128)(2,1)S(1)}, u32[]{:S(2)}, u32[]{:S(2)}) collective-permute-start(bf16[2,2,4,16,512]{4,3,2,1,0:T(8,128)(2,1)S(1)} %add_convert_fusion), channel_id=1, source_target_pairs={{0,4},{1,5},{2,6},{3,7},{4,0},{5,1},{6,2},{7,3},{8,12},{9,13},{10,... | collective-permute-start | bytes 786440 | tf_op jit(solution)/shard_map/ppermute | solution.py:387
  69.2 7.5 %collective-permute-start.5 = (bf16[4,1,4,16,512]{4,3,2,1,0:T(8,128)(2,1)S(1)}, bf16[4,1,4,16,512]{4,3,2,1,0:T(8,128)(2,1)S(1)}, u32[]{:S(2)}, u32[]{:S(2)}) collective-permute-start(bf16[4,1,4,16,512]{4,3,2,1,0:T(8,128)(2,1)S(1)} %get-tuple-element.25), channel_id=1, source_target_pairs={{0,1},{1,0},{2,3},{3,2},{4,5},{5,4},{6,7},{7,6},{8,9},{9,8},{10,11... | collective-permute-start | bytes 786440 | tf_op jit(solution)/shard_map/ppermute | solution.py:387
  70.9 6.9 %collective-permute-start.13 = (bf16[1,1,4,16,512]{4,3,2,1,0:T(8,128)(2,1)S(1)}, bf16[1,1,4,16,512]{4,3,2,1,0:T(8,128)(2,1)S(1)}, u32[]{:S(2)}, u32[]{:S(2)}) collective-permute-start(bf16[1,1,4,16,512]{4,3,2,1,0:T(8,128)(2,1)S(1)} %get-tuple-element.33), channel_id=1, source_target_pairs={{0,6},{1,7},{2,4},{3,5},{4,2},{5,3},{6,0},{7,1},{8,14},{9,15},{10,... | collective-permute-start | bytes 196616 | tf_op jit(solution)/shard_map/ppermute | solution.py:387
  72.9 6.2 %collective-permute-start.12 = (bf16[1,1,4,16,512]{4,3,2,1,0:T(8,128)(2,1)S(1)}, bf16[1,1,4,16,512]{4,3,2,1,0:T(8,128)(2,1)S(1)}, u32[]{:S(2)}, u32[]{:S(2)}) collective-permute-start(bf16[1,1,4,16,512]{4,3,2,1,0:T(8,128)(2,1)S(1)} %get-tuple-element.34), channel_id=1, source_target_pairs={{0,4},{1,5},{2,6},{3,7},{4,0},{5,1},{6,2},{7,3},{8,12},{9,13},{10,... | collective-permute-start | bytes 196616 | tf_op jit(solution)/shard_map/ppermute | solution.py:387
  74.6 6.7 %collective-permute-start.11 = (bf16[1,1,4,16,512]{4,3,2,1,0:T(8,128)(2,1)S(1)}, bf16[1,1,4,16,512]{4,3,2,1,0:T(8,128)(2,1)S(1)}, u32[]{:S(2)}, u32[]{:S(2)}) collective-permute-start(bf16[1,1,4,16,512]{4,3,2,1,0:T(8,128)(2,1)S(1)} %get-tuple-element.35), channel_id=1, source_target_pairs={{0,2},{1,3},{2,0},{3,1},{4,6},{5,7},{6,4},{7,5},{8,10},{9,11},{10,... | collective-permute-start | bytes 196616 | tf_op jit(solution)/shard_map/ppermute | solution.py:387
  75.4 5.8 %collective-permute-start.9 = (bf16[1,2,4,16,512]{4,3,2,1,0:T(8,128)(2,1)S(1)}, bf16[1,2,4,16,512]{4,3,2,1,0:T(8,128)(2,1)S(1)}, u32[]{:S(2)}, u32[]{:S(2)}) collective-permute-start(bf16[1,2,4,16,512]{4,3,2,1,0:T(8,128)(2,1)S(1)} %add_convert_fusion.1), channel_id=1, source_target_pairs={{0,2},{1,3},{2,0},{3,1},{4,6},{5,7},{6,4},{7,5},{8,10},{9,11},{10,... | collective-permute-start | bytes 393224 | tf_op jit(solution)/shard_map/ppermute | solution.py:387
  76.8 6.2 %collective-permute-start.8 = (bf16[1,1,4,16,512]{4,3,2,1,0:T(8,128)(2,1)S(1)}, bf16[1,1,4,16,512]{4,3,2,1,0:T(8,128)(2,1)S(1)}, u32[]{:S(2)}, u32[]{:S(2)}) collective-permute-start(bf16[1,1,4,16,512]{4,3,2,1,0:T(8,128)(2,1)S(1)} %get-tuple-element.36), channel_id=1, source_target_pairs={{0,6},{1,7},{2,4},{3,5},{4,2},{5,3},{6,0},{7,1},{8,14},{9,15},{10,... | collective-permute-start | bytes 196616 | tf_op jit(solution)/shard_map/ppermute | solution.py:387
  77.8 6.5 %collective-permute-start.7 = (bf16[1,1,4,16,512]{4,3,2,1,0:T(8,128)(2,1)S(1)}, bf16[1,1,4,16,512]{4,3,2,1,0:T(8,128)(2,1)S(1)}, u32[]{:S(2)}, u32[]{:S(2)}) collective-permute-start(bf16[1,1,4,16,512]{4,3,2,1,0:T(8,128)(2,1)S(1)} %get-tuple-element.37), channel_id=1, source_target_pairs={{0,4},{1,5},{2,6},{3,7},{4,0},{5,1},{6,2},{7,3},{8,12},{9,13},{10,... | collective-permute-start | bytes 196616 | tf_op jit(solution)/shard_map/ppermute | solution.py:387
  79.1 5.2 %collective-permute-start.6 = (bf16[1,1,4,16,512]{4,3,2,1,0:T(8,128)(2,1)S(1)}, bf16[1,1,4,16,512]{4,3,2,1,0:T(8,128)(2,1)S(1)}, u32[]{:S(2)}, u32[]{:S(2)}) collective-permute-start(bf16[1,1,4,16,512]{4,3,2,1,0:T(8,128)(2,1)S(1)} %get-tuple-element.38), channel_id=1, source_target_pairs={{0,2},{1,3},{2,0},{3,1},{4,6},{5,7},{6,4},{7,5},{8,10},{9,11},{10,... | collective-permute-start | bytes 196616 | tf_op jit(solution)/shard_map/ppermute | solution.py:387
where the time goes:
time: 84.5 us; the launch traced here: 85 us
  Pallas kernels  48.9 us (58%)
  starting transfers between devices  25 us (30%)
  waiting for transfers between devices  6.74 us (8%)
  other arithmetic  3.54 us (4%)
    ppermute x14, starting transfers between devices, exchange(): return lax.ppermute(value, 'vis', [(i, i ^ bits) for i in range(devices)])  25 us
    pallas_call x2, Pallas kernels, local(): pl.pallas_call(functools.partial(later_kernel, facet, (facet - FIRST) * N...  24.5 us
    pallas_call x1, Pallas kernels, local(): pl.pallas_call(functools.partial(first_kernel, FIRST, LISTS * stride, row...  22.8 us
    ppermute x14, waiting for transfers between devices, exchange(): return lax.ppermute(value, 'vis', [(i, i ^ bits) for i in range(devices)])  6.74 us
  transfers between devices with their start and end apart: 14, of which 5 were waited for; matrix products, arithmetic and copies ran while one was open for 0% of the time, Pallas kernels for 30%

commit v1 on v0

--- a/solution.py
+++ b/solution.py
@@ -24,8 +24,8 @@
 LISTS = F - FIRST + 1
 SPARE = FIRST * NP
 GAIN = 0.5
-VMEM_BYTES = 60 * 1024 * 1024
-LATER_VMEM = 52 * 1024 * 1024
+FIRST_VMEM = 53 * 1024 * 1024
+LATER_VMEM = 53 * 1024 * 1024
 FINAL_VMEM = 6 * 1024 * 1024
 
 BF16 = jnp.bfloat16
@@ -95,6 +95,18 @@
     return half(by_columns(np.concatenate(parts, axis=1).reshape(2 * P_SIZE, P_SIZE) * weight))
 
 
+def small_tables(weight):
+    lanes, rows = flip_tables()
+    columns = inverse_column_table(weight).reshape(SIDE * SIDE, PAIR, S)
+    return np.concatenate([lanes, rows, inverse_row_tables(), columns])
+
+
+def inverse_columns(ref, chunk):
+    first = 4 + 2 * SIDE
+    parts = [ref[first + SIDE * k : first + SIDE * (k + 1)].reshape(2 * P_SIZE, S) for k in (chunk, chunk + 1)]
+    return jnp.concatenate(parts, axis=1)
+
+
 def dot(a, b):
     return jnp.dot(a, b, preferred_element_type=F32)
 
@@ -109,7 +121,7 @@
     return jnp.concatenate([pair[:, :S], pair[:, S:]], axis=0)
 
 
-def prepare(slot_ref, plane_ref, count_ref, wk_ref, vis_ref, sky_ref, row_ref, gram_ref, half_ref, kern, kern_t, acc, held, loads, leave):
+def prepare(spot_ref, count_ref, wk_ref, vis_ref, sky_ref, row_ref, gram_ref, half_ref, kern, kern_t, acc, held, loads, leave):
     acc[...] = jnp.zeros_like(acc)
     loads[0].wait()
     for load in loads[4:]:
@@ -125,7 +137,9 @@
         )
         kern[w] = block
         kern_t[w] = block_t
-        gram_ref[w] = dot(block_t, block).astype(BF16)
+        part = dot(block_t, block[:, :S]).astype(BF16)
+        turned = jnp.concatenate([-part[S:], part[:S]], axis=0)
+        gram_ref[w] = jnp.concatenate([part, turned], axis=1)
     leave[0].start()
 
     loads[1].wait()
@@ -141,13 +155,13 @@
         t = jnp.minimum(n * PREP_UNROLL + lane, TILE_CAP - 1)
         alive = jnp.where(n * PREP_UNROLL + lane < count, 1.0, 0.0).astype(F32)
         observed = jnp.concatenate([vis_ref[t, 0], vis_ref[t, 1]], axis=1)
-        right = (dot(observed, kern[plane_ref[t]]) * alive).astype(BF16)
+        right = (dot(observed, kern[spot_ref[t] >> 8]) * alive).astype(BF16)
         held[lane, :, :S] = turn_pair(right)
 
     def left_product(n, lane):
         t = jnp.minimum(n * PREP_UNROLL + lane, TILE_CAP - 1)
-        slot = slot_ref[t]
-        both = dot(kern_t[plane_ref[t]], held[lane, :, :S])
+        slot = spot_ref[t] & 255
+        both = dot(kern_t[spot_ref[t] >> 8], held[lane, :, :S])
         acc[slot] = acc[slot] + jnp.concatenate([both[:S], both[S:]], axis=1)
 
     def step(n, carry):
@@ -198,8 +212,7 @@
 def both_cycles(
     facets, coef, base, times, count, pos, devices, items_ref, gram_ref, back_ref, half_of, tables, grid, acc, flip, held, keep_ref, send_ref
 ):
-    column_ref, lanes_ref, rows_ref, inv_row_ref, inv_col_ref = tables[:5]
-    loads = tables[5]
+    column_ref, table_ref, loads = tables
 
     def block(ref, facet, pc):
         first = facet * NP + pc * SIDE
@@ -219,12 +232,12 @@
         for pc in range(SIDE):
             place(grid, facet, pc, column_pass(0, facet, pc).astype(BF16))
     if loads[0] is not None:
-        loads[7].wait()
+        loads[4].wait()
         acc[:NP] = back_ref[...].astype(F32)
         loads[0].wait()
     degrid_grid(items_ref, base, times, count, gram_ref, grid, acc, held)
 
-    for load in loads[2:5]:
+    for load in loads[2:4]:
         if load is not None:
             load.wait()
     lane = lax.broadcasted_iota(jnp.int32, (1, PAIR), 1)
@@ -234,7 +247,7 @@
         for pc in range(SIDE):
             place(flip, facet, pc, block(acc, facet, pc).astype(BF16))
         for pc in range(SIDE):
-            turned = dot(block(flip, facet, SIDE - 1 - pc), wide(lanes_ref, 0))
+            turned = dot(block(flip, facet, SIDE - 1 - pc), wide(table_ref, 0))
             edge = block(flip, facet, (SIDE - pc) % SIDE).astype(F32) * sign
             mirrored = jnp.where(lane % S == 0, edge, turned)
             mirrored_half = mirrored.astype(BF16)
@@ -244,7 +257,7 @@
             for b in range(2):
                 mine = slice(b * PAIR, (b + 1) * PAIR)
                 other = slice((1 - b) * PAIR, (2 - b) * PAIR)
-                swapped = dot(wide(rows_ref, 0), mirrored_half[other])
+                swapped = dot(wide(table_ref, 2), mirrored_half[other])
                 swapped = jnp.where(row == 0, mirrored[mine], swapped)
                 parts.append((fresh[mine] + coef * (own[mine] + swapped)).astype(BF16))
             place(grid, facet, pc, jnp.concatenate(parts, axis=0))
@@ -253,8 +266,6 @@
             place(acc, facet, pc, block(back_ref, facet, pc).astype(F32))
     degrid_grid(items_ref, base, times, count, gram_ref, grid, acc, held)
 
-    loads[5].wait()
-    loads[6].wait()
     share, far = S // devices, devices // 2
     for facet in range(facets):
         mixed = [[] for _ in range(SIDE)]
@@ -266,12 +277,12 @@
             for q, value in enumerate((even + even_b, odd + turned, even - even_b, odd - turned)):
                 mixed[q].append(turn_pair(value.astype(BF16)))
         for q in range(SIDE):
-            spec = dot(wide(inv_row_ref, 2 * q), jnp.concatenate(mixed[q], axis=1)).astype(BF16)
+            spec = dot(wide(table_ref, 4 + 2 * q), jnp.concatenate(mixed[q], axis=1)).astype(BF16)
             for pc in range(SIDE):
                 cols = slice(pc * S, (pc + 1) * S)
                 flip[facet * NP + pc * SIDE + q] = jnp.concatenate([spec[:S, cols], spec[S:, cols]], axis=1)
         spec = jnp.concatenate([block(flip, facet, pc) for pc in range(SIDE)], axis=1)
-        image = jnp.concatenate([dot(spec, wide(inv_col_ref, j)) for j in range(0, SIDE, 2)], axis=1).astype(BF16)
+        image = jnp.concatenate([dot(spec, inverse_columns(table_ref, j)) for j in range(0, SIDE, 2)], axis=1).astype(BF16)
         for q in range(SIDE):
             part = image[q * S : (q + 1) * S]
             if send_ref is None:
@@ -291,13 +302,13 @@
 
 
 def first_kernel(facets, times, rows, coef, devices, outs, *refs):
-    pos_ref, items_ref, slot_ref, plane_ref, live_ref = refs[:5]
-    wk_hbm, vis_hbm, sky_hbm, row_hbm, column_hbm, *table_hbm = refs[5:14]
-    gram_hbm, back_hbm, half_hbm, *images = refs[14 : 17 + outs]
-    wk_ref, vis_ref, sky_ref, row_ref, column_ref, *table_refs = refs[17 + outs : 26 + outs]
-    gram_ref, half_ref, back_ref, kern, kern_t, acc, grid, flip, held, sems = refs[26 + outs :]
+    pos_ref, items_ref, spot_ref, live_ref = refs[:4]
+    wk_hbm, vis_hbm, sky_hbm, row_hbm, column_hbm, table_hbm = refs[4:10]
+    gram_hbm, back_hbm, half_hbm, *images = refs[10 : 13 + outs]
+    wk_ref, vis_ref, sky_ref, row_ref, column_ref, table_ref = refs[13 + outs : 19 + outs]
+    gram_ref, half_ref, back_ref, kern, kern_t, acc, grid, flip, held, sems = refs[19 + outs :]
     moves = [(wk_hbm, wk_ref), (sky_hbm, sky_ref), (row_hbm, row_ref), (vis_hbm, vis_ref), (column_hbm.at[pos_ref[0]], column_ref)]
-    loads = copies(moves + list(zip(table_hbm, table_refs)), sems)
+    loads = copies(moves + [(table_hbm, table_ref)], sems)
     for load in loads[:4]:
         load.start()
     later = facets * NP
@@ -305,7 +316,7 @@
         [(gram_ref, gram_hbm), (half_ref, half_hbm), (back_ref.at[pl.ds(later, F * NP - later)], back_hbm)], sems, len(loads)
     )
     prepare(
-        slot_ref, plane_ref, live_ref, wk_ref, vis_ref, sky_ref, row_ref, gram_ref, half_ref, kern, kern_t, acc, held, loads, leave
+        spot_ref, live_ref, wk_ref, vis_ref, sky_ref, row_ref, gram_ref, half_ref, kern, kern_t, acc, held, loads, leave
     )
     for slot in range(0, F * NP, NP):
         back_ref[slot : slot + NP] = acc[slot : slot + NP].astype(BF16)
@@ -315,7 +326,7 @@
         first = (cycle * F + facet) * rows
         return half_ref[first : first + rows, pc * PAIR : (pc + 1) * PAIR]
 
-    tables = (column_ref, *table_refs, [None, loads[4], None, *loads[5:]])
+    tables = (column_ref, table_ref, [None, loads[4], None, loads[5]])
     keep_ref, send_ref = images if outs == 2 else (images[0], None)
     both_cycles(
         facets, coef, 0, times, items_ref[2 * times], pos_ref[0], devices, items_ref, gram_ref, back_ref, half_of, tables, grid, acc, flip, held, keep_ref, send_ref
@@ -326,10 +337,10 @@
 
 def later_kernel(facet, offset, base, times, part, rows, coef, devices, outs, *refs):
     pos_ref, items_ref = refs[:2]
-    gram_hbm, back_hbm, half_hbm, column_hbm, *table_hbm = refs[2:10]
-    images = refs[10 : 10 + outs]
-    gram_ref, back_ref, half_ref, column_ref, *table_refs = refs[10 + outs : 18 + outs]
-    acc, grid, flip, held, sems = refs[18 + outs :]
+    gram_hbm, back_hbm, half_hbm, column_hbm, table_hbm = refs[2:7]
+    images = refs[7 : 7 + outs]
+    gram_ref, back_ref, half_ref, column_ref, table_ref = refs[7 + outs : 12 + outs]
+    acc, grid, flip, held, sems = refs[12 + outs :]
     moves = [
         (half_hbm.at[pl.ds(facet * rows, rows)], half_ref.at[0]),
         (column_hbm.at[pos_ref[0]], column_ref),
@@ -337,7 +348,7 @@
         (gram_hbm, gram_ref),
         (half_hbm.at[pl.ds((F + facet) * rows, rows)], half_ref.at[1]),
     ]
-    loads = copies(moves + list(zip(table_hbm, table_refs)), sems)
+    loads = copies(moves + [(table_hbm, table_ref)], sems)
     for load in loads[:4]:
         load.start()
     for load in loads[4:]:
@@ -347,7 +358,7 @@
     def half_of(cycle, _, pc):
         return half_ref[cycle, :, pc * PAIR : (pc + 1) * PAIR]
 
-    tables = (column_ref, *table_refs, [loads[3], loads[1], *loads[4:], loads[2]])
+    tables = (column_ref, table_ref, [loads[3], loads[1], loads[4], loads[5], loads[2]])
     keep_ref, send_ref = images if outs == 2 else (images[0], None)
     both_cycles(
         1, coef, base, times, items_ref[2 * times + part], pos_ref[0], devices, items_ref, gram_ref, back_ref, half_of, tables, grid, acc, flip, held, keep_ref, send_ref
@@ -435,9 +446,7 @@
         bits *= 2
     items = tile_lists(codes, stride)
 
-    lanes, row_flip = flip_tables()
-    tables = [column_tables(devices), lanes, row_flip, inverse_row_tables(), inverse_column_table(weight)]
-    tables = [jnp.asarray(t) for t in tables]
+    tables = [jnp.asarray(column_tables(devices)), jnp.asarray(small_tables(weight))]
     here = position.reshape(1)
     smem = pl.BlockSpec(memory_space=pltpu.SMEM)
     vmem = pl.BlockSpec(memory_space=pltpu.VMEM)
@@ -453,11 +462,11 @@
     def halves_of(images):
         return images if split else split_image(images[0], position, devices)
 
-    params = pltpu.CompilerParams(vmem_limit_bytes=VMEM_BYTES)
+    params = pltpu.CompilerParams(vmem_limit_bytes=FIRST_VMEM)
     outs = 2 if split else 1
     half_shape = (2 * F * rows, 2 * P_SIZE)
     gram_shape = (WPLANES, PAIR, PAIR)
-    table_scratch = [pltpu.VMEM((P_SIZE, 2 * rows), BF16)] + [pltpu.VMEM(t.shape, BF16) for t in tables[1:]]
+    table_scratch = [pltpu.VMEM((P_SIZE, 2 * rows), BF16), pltpu.VMEM(tables[1].shape, BF16)]
 
     gram, back, half_rows, *images = pl.pallas_call(
         functools.partial(first_kernel, FIRST, LISTS * stride, rows, coef, devices, outs),
@@ -467,7 +476,7 @@
             jax.ShapeDtypeStruct(half_shape, BF16),
             *image_shapes(FIRST),
         ],
-        in_specs=[smem] * 5 + [hbm] * 9,
+        in_specs=[smem] * 4 + [hbm] * 6,
         out_specs=[hbm] * 3 + [vmem] * outs,
         scratch_shapes=[
             pltpu.VMEM(w_kernels.shape, BF16),
@@ -492,8 +501,7 @@
     )(
         here,
         items,
-        slots,
-        tile_wplane,
+        slots + (tile_wplane << 8),
         tile_count,
         w_kernels,
         visibilities,
@@ -520,7 +528,7 @@
                 later_kernel, facet, (facet - FIRST) * NP, part * stride, LISTS * stride, part, rows, coef, devices, outs
             ),
             out_shape=image_shapes(1),
-            in_specs=[smem] * 2 + [hbm] * 8,
+            in_specs=[smem] * 2 + [hbm] * 5,
             out_specs=[vmem] * outs,
             scratch_shapes=[
                 pltpu.VMEM(gram_shape, BF16),

time: 84.5 us -> 84.5 us (level); the launches traced: 85 us -> 84.1 us
  waiting for transfers between devices: 6.74 us -> 9.03 us
  starting transfers between devices: 25 us -> 23.1 us
  other arithmetic: 3.54 us -> 2.4 us
    ppermute x14, waiting for transfers between devices: 6.74 us -> 9.03 us  [exchange(): return lax.ppermute(value, 'vis', [(i, i ^ bits) for i in range(devices)])]
    ppermute x14, starting transfers between devices: 25 us -> 23.1 us  [exchange(): return lax.ppermute(value, 'vis', [(i, i ^ bits) for i in range(devices)])]
    pallas_call x2, Pallas kernels: 24.5 us -> 23.6 us  [local(): pl.pallas_call(functools.partial(later_kernel, facet, (facet - FIRST) * N...]
  transfers between devices with their start and end apart: 14 -> 14, of which waited for: 5 -> 8; matrix products, arithmetic and copies ran while one was open for 0% -> 0% of each run, Pallas kernels for 30% -> 29%
where the time goes in v1:
time: 84.5 us; the launch traced here: 84.1 us
  Pallas kernels  48.7 us (58%)
  starting transfers between devices  23.1 us (27%)
  waiting for transfers between devices  9.03 us (11%)
  other arithmetic  2.4 us (3%)
    pallas_call x2, Pallas kernels, local(): pl.pallas_call(functools.partial(later_kernel, facet, (facet - FIRST) * N...  23.6 us
    pallas_call x1, Pallas kernels, local(): pl.pallas_call(functools.partial(first_kernel, FIRST, LISTS * stride, row...  23.5 us
    ppermute x14, starting transfers between devices, exchange(): return lax.ppermute(value, 'vis', [(i, i ^ bits) for i in range(devices)])  23.1 us
    ppermute x14, waiting for transfers between devices, exchange(): return lax.ppermute(value, 'vis', [(i, i ^ bits) for i in range(devices)])  9.03 us
  transfers between devices with their start and end apart: 14, of which 8 were waited for; matrix products, arithmetic and copies ran while one was open for 0% of the time, Pallas kernels for 29%

profile of v1, /device:TPU:0, one launch (start us, length us, event | category | flops | bytes accessed | tf_op | source)
XLA Modules:
  0.0 84.1 jit_solution(12319990196694003033)
XLA Ops:
  0.7 0.7 shift-left_add_fusion
  1.4 3.0 %collective-permute-start = (s32[32]{0:T(128)S(1)}, s32[32]{0:T(128)S(1)}, u32[]{:S(2)}, u32[]{:S(2)}) collective-permute-start(s32[32]{0:T(128)S(1)} %get-tuple-element.40), channel_id=1, source_target_pairs={{0,1},{1,0},{2,3},{3,2},{4,5},{5,4},{6,7},{7,6},{8,9},{9,8},{10,11... | collective-permute-start | bytes 392 | tf_op jit(solution)/shard_map/ppermute | solution.py:398
  4.3 1.5 %collective-permute-done = s32[32]{0:T(128)S(1)} collective-permute-done((s32[32]{0:T(128)S(1)}, s32[32]{0:T(128)S(1)}, u32[]{:S(2)}, u32[]{:S(2)}) %collective-permute-start) | collective-permute-done | bytes 160 | tf_op jit(solution)/shard_map/ppermute | solution.py:398
  5.9 2.1 %collective-permute-start.1 = (s32[64]{0:T(128)S(1)}, s32[64]{0:T(128)S(1)}, u32[]{:S(2)}, u32[]{:S(2)}) collective-permute-start(s32[64]{0:T(128)S(1)} %pad_add_fusion.1), channel_id=1, source_target_pairs={{0,2},{1,3},{2,0},{3,1},{4,6},{5,7},{6,4},{7,5},{8,10},{9,11},{10,... | collective-permute-start | bytes 776 | tf_op jit(solution)/shard_map/ppermute | solution.py:398
  8.0 1.5 %collective-permute-done.1 = s32[64]{0:T(128)S(1)} collective-permute-done((s32[64]{0:T(128)S(1)}, s32[64]{0:T(128)S(1)}, u32[]{:S(2)}, u32[]{:S(2)}) %collective-permute-start.1) | collective-permute-done | bytes 288 | tf_op jit(solution)/shard_map/ppermute | solution.py:398
  9.6 3.0 %collective-permute-start.2 = (s32[128]{0:T(128)S(1)}, s32[128]{0:T(128)S(1)}, u32[]{:S(2)}, u32[]{:S(2)}) collective-permute-start(s32[128]{0:T(128)S(1)} %pad_add_fusion.2), channel_id=1, source_target_pairs={{0,4},{1,5},{2,6},{3,7},{4,0},{5,1},{6,2},{7,3},{8,12},{9,13},{10,... | collective-permute-start | bytes 1544 | tf_op jit(solution)/shard_map/ppermute | solution.py:398
  12.6 1.5 %collective-permute-done.2 = s32[128]{0:T(128)S(1)} collective-permute-done((s32[128]{0:T(128)S(1)}, s32[128]{0:T(128)S(1)}, u32[]{:S(2)}, u32[]{:S(2)}) %collective-permute-start.2) | collective-permute-done | bytes 544 | tf_op jit(solution)/shard_map/ppermute | solution.py:398
  15.5 23.5 %first.1 = (bf16[16,256,256]{2,1,0:T(8,128)(2,1)}, bf16[32,128,256]{2,1,0:T(8,128)(2,1)}, bf16[512,1024]{1,0:T(8,128)(2,1)}, bf16[4,2,4,16,512]{4,3,2,1,0:T(8,128)(2,1)S(1)}, bf16[4,2,4,16,512]{4,3,2,1,0:T(8,128)(2,1)}) custom-call(s32[1]{0:T(128)} %bitcast.refs_0_, s32[855]{0:T(1024)S(1)} %select_add_fusion.refs_1_, s32[32]{0:T(128)S(1)} %get-tuple-element.39.refs_2_, ...), custom_call_target="tpu_custom_call" | custom-call | flops 30000001024 | bytes 12582912 | tf_op jit(solution)/shard_map/first/pallas_call | solution.py:471
  39.0 2.5 %collective-permute-start.3 = (bf16[4,2,4,16,512]{4,3,2,1,0:T(8,128)(2,1)}, bf16[4,2,4,16,512]{4,3,2,1,0:T(8,128)(2,1)S(1)}, u32[]{:S(2)}, u32[]{:S(2)}) collective-permute-start(bf16[4,2,4,16,512]{4,3,2,1,0:T(8,128)(2,1)} %get-tuple-element.18), channel_id=1, source_target_pairs={{0,1},{1,0},{2,3},{3,2},{4,5},{5,4},{6,7},{7,6},{8,9},{9,8},{10,11... | collective-permute-start | bytes 1572872 | tf_op jit(solution)/shard_map/ppermute | solution.py:398
  41.5 12.9 %facet.3 = (bf16[4,1,4,16,512]{4,3,2,1,0:T(8,128)(2,1)S(1)}, bf16[4,1,4,16,512]{4,3,2,1,0:T(8,128)(2,1)S(1)}) custom-call(s32[1]{0:T(128)} %bitcast.refs_0_, s32[855]{0:T(1024)S(1)} %select_add_fusion.refs_1_, bf16[16,256,256]{2,1,0:T(8,128)(2,1)} %get-tuple-element.20.refs_2_, bf16[32,128,256]{2,1,0:T(8,128)(2,1)} %get-tuple-element.21.refs_3_, ...), custom_call_target="tpu_custom_call" | custom-call | flops 14000000000 | bytes 6291456 | tf_op jit(solution)/shard_map/facet/pallas_call | solution.py:526
  54.6 2.7 %collective-permute-start.4 = (bf16[2,2,4,16,512]{4,3,2,1,0:T(8,128)(2,1)S(1)}, bf16[2,2,4,16,512]{4,3,2,1,0:T(8,128)(2,1)S(1)}, u32[]{:S(2)}, u32[]{:S(2)}) collective-permute-start(bf16[2,2,4,16,512]{4,3,2,1,0:T(8,128)(2,1)S(1)} %add_convert_fusion), channel_id=1, source_target_pairs={{0,4},{1,5},{2,6},{3,7},{4,0},{5,1},{6,2},{7,3},{8,12},{9,13},{10,... | collective-permute-start | bytes 786440 | tf_op jit(solution)/shard_map/ppermute | solution.py:398
  57.2 10.7 %facet.2 = (bf16[4,1,4,16,512]{4,3,2,1,0:T(8,128)(2,1)S(1)}, bf16[4,1,4,16,512]{4,3,2,1,0:T(8,128)(2,1)S(1)}) custom-call(s32[1]{0:T(128)} %bitcast.refs_0_, s32[855]{0:T(1024)S(1)} %select_add_fusion.refs_1_, bf16[16,256,256]{2,1,0:T(8,128)(2,1)} %get-tuple-element.20.refs_2_, bf16[32,128,256]{2,1,0:T(8,128)(2,1)} %get-tuple-element.21.refs_3_, ...), custom_call_target="tpu_custom_call" | custom-call | flops 14000000000 | bytes 6291456 | tf_op jit(solution)/shard_map/facet/pallas_call | solution.py:526
  68.0 2.1 %collective-permute-start.5 = (bf16[4,1,4,16,512]{4,3,2,1,0:T(8,128)(2,1)S(1)}, bf16[4,1,4,16,512]{4,3,2,1,0:T(8,128)(2,1)S(1)}, u32[]{:S(2)}, u32[]{:S(2)}) collective-permute-start(bf16[4,1,4,16,512]{4,3,2,1,0:T(8,128)(2,1)S(1)} %get-tuple-element.25), channel_id=1, source_target_pairs={{0,1},{1,0},{2,3},{3,2},{4,5},{5,4},{6,7},{7,6},{8,9},{9,8},{10,11... | collective-permute-start | bytes 786440 | tf_op jit(solution)/shard_map/ppermute | solution.py:398
  70.1 1.4 %collective-permute-start.13 = (bf16[1,1,4,16,512]{4,3,2,1,0:T(8,128)(2,1)S(1)}, bf16[1,1,4,16,512]{4,3,2,1,0:T(8,128)(2,1)S(1)}, u32[]{:S(2)}, u32[]{:S(2)}) collective-permute-start(bf16[1,1,4,16,512]{4,3,2,1,0:T(8,128)(2,1)S(1)} %get-tuple-element.33), channel_id=1, source_target_pairs={{0,6},{1,7},{2,4},{3,5},{4,2},{5,3},{6,0},{7,1},{8,14},{9,15},{10,... | collective-permute-start | bytes 196616 | tf_op jit(solution)/shard_map/ppermute | solution.py:398
  71.5 1.1 %collective-permute-start.12 = (bf16[1,1,4,16,512]{4,3,2,1,0:T(8,128)(2,1)S(1)}, bf16[1,1,4,16,512]{4,3,2,1,0:T(8,128)(2,1)S(1)}, u32[]{:S(2)}, u32[]{:S(2)}) collective-permute-start(bf16[1,1,4,16,512]{4,3,2,1,0:T(8,128)(2,1)S(1)} %get-tuple-element.34), channel_id=1, source_target_pairs={{0,4},{1,5},{2,6},{3,7},{4,0},{5,1},{6,2},{7,3},{8,12},{9,13},{10,... | collective-permute-start | bytes 196616 | tf_op jit(solution)/shard_map/ppermute | solution.py:398
  72.6 1.9 %collective-permute-start.11 = (bf16[1,1,4,16,512]{4,3,2,1,0:T(8,128)(2,1)S(1)}, bf16[1,1,4,16,512]{4,3,2,1,0:T(8,128)(2,1)S(1)}, u32[]{:S(2)}, u32[]{:S(2)}) collective-permute-start(bf16[1,1,4,16,512]{4,3,2,1,0:T(8,128)(2,1)S(1)} %get-tuple-element.35), channel_id=1, source_target_pairs={{0,2},{1,3},{2,0},{3,1},{4,6},{5,7},{6,4},{7,5},{8,10},{9,11},{10,... | collective-permute-start | bytes 196616 | tf_op jit(solution)/shard_map/ppermute | solution.py:398
  74.8 1.5 %collective-permute-start.8 = (bf16[1,1,4,16,512]{4,3,2,1,0:T(8,128)(2,1)S(1)}, bf16[1,1,4,16,512]{4,3,2,1,0:T(8,128)(2,1)S(1)}, u32[]{:S(2)}, u32[]{:S(2)}) collective-permute-start(bf16[1,1,4,16,512]{4,3,2,1,0:T(8,128)(2,1)S(1)} %get-tuple-element.36), channel_id=1, source_target_pairs={{0,6},{1,7},{2,4},{3,5},{4,2},{5,3},{6,0},{7,1},{8,14},{9,15},{10,... | collective-permute-start | bytes 196616 | tf_op jit(solution)/shard_map/ppermute | solution.py:398
  76.9 1.4 %collective-permute-start.7 = (bf16[1,1,4,16,512]{4,3,2,1,0:T(8,128)(2,1)S(1)}, bf16[1,1,4,16,512]{4,3,2,1,0:T(8,128)(2,1)S(1)}, u32[]{:S(2)}, u32[]{:S(2)}) collective-permute-start(bf16[1,1,4,16,512]{4,3,2,1,0:T(8,128)(2,1)S(1)} %get-tuple-element.37), channel_id=1, source_target_pairs={{0,4},{1,5},{2,6},{3,7},{4,0},{5,1},{6,2},{7,3},{8,12},{9,13},{10,... | collective-permute-start | bytes 196616 | tf_op jit(solution)/shard_map/ppermute | solution.py:398
  78.3 0.8 collective-permute-done.12.refs_7_
  79.3 1.1 %collective-permute-done.9.refs_3_ = bf16[1,2,4,16,512]{4,3,2,1,0:T(8,128)(2,1)S(1)} collective-permute-done((bf16[1,2,4,16,512]{4,3,2,1,0:T(8,128)(2,1)S(1)}, bf16[1,2,4,16,512]{4,3,2,1,0:T(8,128)(2,1)S(1)}, u32[]{:S(2)}, u32[]{:S(2)}) %collective-permute-start.9) | collective-permute-done | bytes 131104 | tf_op jit(solution)/shard_map/ppermute | solution.py:398
  80.4 0.9 %final.2.refs_5_ = f32[4,64,512]{2,1,0:T(8,128)} custom-call(bf16[4,2,4,16,512]{4,3,2,1,0:T(8,128)(2,1)S(1)} %get-tuple-element.17.refs_0_, bf16[4,2,4,16,512]{4,3,2,1,0:T(8,128)(2,1)S(1)} %collective-permute-done.3.refs_1_, bf16[2,2,4,16,512]{4,3,2,1,0:T(8,128)(2,1)S(1)} %collective-permute-done.4.refs_2_, ...), custom_call_target="tpu_custom_call" | custom-call | flops 1000000 | bytes 1048576 | tf_op jit(solution)/shard_map/final/pallas_call | solution.py:563
  81.3 0.7 collective-permute-done.7.refs_3_
  82.0 1.3 %collective-permute-done.6.refs_2_ = bf16[1,1,4,16,512]{4,3,2,1,0:T(8,128)(2,1)S(1)} collective-permute-done((bf16[1,1,4,16,512]{4,3,2,1,0:T(8,128)(2,1)S(1)}, bf16[1,1,4,16,512]{4,3,2,1,0:T(8,128)(2,1)S(1)}, u32[]{:S(2)}, u32[]{:S(2)}) %collective-permute-start.6) | collective-permute-done | bytes 65568 | tf_op jit(solution)/shard_map/ppermute | solution.py:398
  83.3 0.7 final.3
  (31 shorter events, 2.7 us)
Async XLA Ops:
  1.4 4.5 %collective-permute-start = (s32[32]{0:T(128)S(1)}, s32[32]{0:T(128)S(1)}, u32[]{:S(2)}, u32[]{:S(2)}) collective-permute-start(s32[32]{0:T(128)S(1)} %get-tuple-element.40), channel_id=1, source_target_pairs={{0,1},{1,0},{2,3},{3,2},{4,5},{5,4},{6,7},{7,6},{8,9},{9,8},{10,11... | collective-permute-start | bytes 392 | tf_op jit(solution)/shard_map/ppermute | solution.py:398
  5.9 3.6 %collective-permute-start.1 = (s32[64]{0:T(128)S(1)}, s32[64]{0:T(128)S(1)}, u32[]{:S(2)}, u32[]{:S(2)}) collective-permute-start(s32[64]{0:T(128)S(1)} %pad_add_fusion.1), channel_id=1, source_target_pairs={{0,2},{1,3},{2,0},{3,1},{4,6},{5,7},{6,4},{7,5},{8,10},{9,11},{10,... | collective-permute-start | bytes 776 | tf_op jit(solution)/shard_map/ppermute | solution.py:398
  9.6 4.6 %collective-permute-start.2 = (s32[128]{0:T(128)S(1)}, s32[128]{0:T(128)S(1)}, u32[]{:S(2)}, u32[]{:S(2)}) collective-permute-start(s32[128]{0:T(128)S(1)} %pad_add_fusion.2), channel_id=1, source_target_pairs={{0,4},{1,5},{2,6},{3,7},{4,0},{5,1},{6,2},{7,3},{8,12},{9,13},{10,... | collective-permute-start | bytes 1544 | tf_op jit(solution)/shard_map/ppermute | solution.py:398
  39.0 15.5 %collective-permute-start.3 = (bf16[4,2,4,16,512]{4,3,2,1,0:T(8,128)(2,1)}, bf16[4,2,4,16,512]{4,3,2,1,0:T(8,128)(2,1)S(1)}, u32[]{:S(2)}, u32[]{:S(2)}) collective-permute-start(bf16[4,2,4,16,512]{4,3,2,1,0:T(8,128)(2,1)} %get-tuple-element.18), channel_id=1, source_target_pairs={{0,1},{1,0},{2,3},{3,2},{4,5},{5,4},{6,7},{7,6},{8,9},{9,8},{10,11... | collective-permute-start | bytes 1572872 | tf_op jit(solution)/shard_map/ppermute | solution.py:398
  54.4 15.6 %collective-permute-start.10 = (bf16[4,1,4,16,512]{4,3,2,1,0:T(8,128)(2,1)S(1)}, bf16[4,1,4,16,512]{4,3,2,1,0:T(8,128)(2,1)S(1)}, u32[]{:S(2)}, u32[]{:S(2)}) collective-permute-start(bf16[4,1,4,16,512]{4,3,2,1,0:T(8,128)(2,1)S(1)} %get-tuple-element.28), channel_id=1, source_target_pairs={{0,1},{1,0},{2,3},{3,2},{4,5},{5,4},{6,7},{7,6},{8,9},{9,8},{10,11... | collective-permute-start | bytes 786440 | tf_op jit(solution)/shard_map/ppermute | solution.py:398
  54.6 13.4 %collective-permute-start.4 = (bf16[2,2,4,16,512]{4,3,2,1,0:T(8,128)(2,1)S(1)}, bf16[2,2,4,16,512]{4,3,2,1,0:T(8,128)(2,1)S(1)}, u32[]{:S(2)}, u32[]{:S(2)}) collective-permute-start(bf16[2,2,4,16,512]{4,3,2,1,0:T(8,128)(2,1)S(1)} %add_convert_fusion), channel_id=1, source_target_pairs={{0,4},{1,5},{2,6},{3,7},{4,0},{5,1},{6,2},{7,3},{8,12},{9,13},{10,... | collective-permute-start | bytes 786440 | tf_op jit(solution)/shard_map/ppermute | solution.py:398
  68.0 6.8 %collective-permute-start.5 = (bf16[4,1,4,16,512]{4,3,2,1,0:T(8,128)(2,1)S(1)}, bf16[4,1,4,16,512]{4,3,2,1,0:T(8,128)(2,1)S(1)}, u32[]{:S(2)}, u32[]{:S(2)}) collective-permute-start(bf16[4,1,4,16,512]{4,3,2,1,0:T(8,128)(2,1)S(1)} %get-tuple-element.25), channel_id=1, source_target_pairs={{0,1},{1,0},{2,3},{3,2},{4,5},{5,4},{6,7},{7,6},{8,9},{9,8},{10,11... | collective-permute-start | bytes 786440 | tf_op jit(solution)/shard_map/ppermute | solution.py:398
  70.1 6.8 %collective-permute-start.13 = (bf16[1,1,4,16,512]{4,3,2,1,0:T(8,128)(2,1)S(1)}, bf16[1,1,4,16,512]{4,3,2,1,0:T(8,128)(2,1)S(1)}, u32[]{:S(2)}, u32[]{:S(2)}) collective-permute-start(bf16[1,1,4,16,512]{4,3,2,1,0:T(8,128)(2,1)S(1)} %get-tuple-element.33), channel_id=1, source_target_pairs={{0,6},{1,7},{2,4},{3,5},{4,2},{5,3},{6,0},{7,1},{8,14},{9,15},{10,... | collective-permute-start | bytes 196616 | tf_op jit(solution)/shard_map/ppermute | solution.py:398
  71.5 7.6 %collective-permute-start.12 = (bf16[1,1,4,16,512]{4,3,2,1,0:T(8,128)(2,1)S(1)}, bf16[1,1,4,16,512]{4,3,2,1,0:T(8,128)(2,1)S(1)}, u32[]{:S(2)}, u32[]{:S(2)}) collective-permute-start(bf16[1,1,4,16,512]{4,3,2,1,0:T(8,128)(2,1)S(1)} %get-tuple-element.34), channel_id=1, source_target_pairs={{0,4},{1,5},{2,6},{3,7},{4,0},{5,1},{6,2},{7,3},{8,12},{9,13},{10,... | collective-permute-start | bytes 196616 | tf_op jit(solution)/shard_map/ppermute | solution.py:398
  72.6 6.7 %collective-permute-start.11 = (bf16[1,1,4,16,512]{4,3,2,1,0:T(8,128)(2,1)S(1)}, bf16[1,1,4,16,512]{4,3,2,1,0:T(8,128)(2,1)S(1)}, u32[]{:S(2)}, u32[]{:S(2)}) collective-permute-start(bf16[1,1,4,16,512]{4,3,2,1,0:T(8,128)(2,1)S(1)} %get-tuple-element.35), channel_id=1, source_target_pairs={{0,2},{1,3},{2,0},{3,1},{4,6},{5,7},{6,4},{7,5},{8,10},{9,11},{10,... | collective-permute-start | bytes 196616 | tf_op jit(solution)/shard_map/ppermute | solution.py:398
  74.6 5.8 %collective-permute-start.9 = (bf16[1,2,4,16,512]{4,3,2,1,0:T(8,128)(2,1)S(1)}, bf16[1,2,4,16,512]{4,3,2,1,0:T(8,128)(2,1)S(1)}, u32[]{:S(2)}, u32[]{:S(2)}) collective-permute-start(bf16[1,2,4,16,512]{4,3,2,1,0:T(8,128)(2,1)S(1)} %add_convert_fusion.1), channel_id=1, source_target_pairs={{0,2},{1,3},{2,0},{3,1},{4,6},{5,7},{6,4},{7,5},{8,10},{9,11},{10,... | collective-permute-start | bytes 393224 | tf_op jit(solution)/shard_map/ppermute | solution.py:398
  74.8 6.5 %collective-permute-start.8 = (bf16[1,1,4,16,512]{4,3,2,1,0:T(8,128)(2,1)S(1)}, bf16[1,1,4,16,512]{4,3,2,1,0:T(8,128)(2,1)S(1)}, u32[]{:S(2)}, u32[]{:S(2)}) collective-permute-start(bf16[1,1,4,16,512]{4,3,2,1,0:T(8,128)(2,1)S(1)} %get-tuple-element.36), channel_id=1, source_target_pairs={{0,6},{1,7},{2,4},{3,5},{4,2},{5,3},{6,0},{7,1},{8,14},{9,15},{10,... | collective-permute-start | bytes 196616 | tf_op jit(solution)/shard_map/ppermute | solution.py:398
  76.9 5.2 %collective-permute-start.7 = (bf16[1,1,4,16,512]{4,3,2,1,0:T(8,128)(2,1)S(1)}, bf16[1,1,4,16,512]{4,3,2,1,0:T(8,128)(2,1)S(1)}, u32[]{:S(2)}, u32[]{:S(2)}) collective-permute-start(bf16[1,1,4,16,512]{4,3,2,1,0:T(8,128)(2,1)S(1)} %get-tuple-element.37), channel_id=1, source_target_pairs={{0,4},{1,5},{2,6},{3,7},{4,0},{5,1},{6,2},{7,3},{8,12},{9,13},{10,... | collective-permute-start | bytes 196616 | tf_op jit(solution)/shard_map/ppermute | solution.py:398
  79.1 4.3 %collective-permute-start.6 = (bf16[1,1,4,16,512]{4,3,2,1,0:T(8,128)(2,1)S(1)}, bf16[1,1,4,16,512]{4,3,2,1,0:T(8,128)(2,1)S(1)}, u32[]{:S(2)}, u32[]{:S(2)}) collective-permute-start(bf16[1,1,4,16,512]{4,3,2,1,0:T(8,128)(2,1)S(1)} %get-tuple-element.38), channel_id=1, source_target_pairs={{0,2},{1,3},{2,0},{3,1},{4,6},{5,7},{6,4},{7,5},{8,10},{9,11},{10,... | collective-permute-start | bytes 196616 | tf_op jit(solution)/shard_map/ppermute | solution.py:398
